TPU v7x, 256 devices: a whole 4x4x8 slice. The times are simulated.
256 devices in a mesh: section: 16 (over y, z_lo, core), seq: 16 (over x, z_hi).
Axes of the slice: x: 4, y: 4, z: 8 (z_hi: 4, z_lo: 2; z = z_hi * 2 + z_lo), core: 2. Of those that a mesh axis runs over, the one named last changes fastest.
Arguments:
- stream: bfloat16 [16, 2048, 4096], P('section', 'seq'), may hold values from -6 to 6
- depth_weights: float32 [16, 4], P('section'), may hold values from 0.3 to 1
- depth_reach: int32 [16], P('section'), may hold values from 0 to 3, as said below
- norm_gain: float32 [16, 4096], P('section'), may hold values from 0.1 to 1.9
- qkv_weight: bfloat16 [16, 4096, 32, 3, 128], P('section', None, 'seq'), may hold values from -3 to 3
Outputs:
- layer_input: bfloat16 [16, 2048, 4096], P('section', 'seq')
- attended: bfloat16 [16, 2048, 4096], P('section', 'seq')
Inputs may be any that keep to these rules, and one draw needn't show every extreme that they name: depth_reach[s] is 0 or min(3, s // 4); the last layer carries a depth average and layer 14 does not.
All inputs are finite; a program needn't handle non-finite values.
Results may differ from a plain program's by a relative error of at most 0.0083.
Values may be sent and summed in bfloat16 or wider, within the bound.
A program may use at most 128 MiB of HBM per device.

v0:
```python
import jax
import jax.numpy as jnp
from jax import lax
from jax.sharding import PartitionSpec as P


def shifted(shard, axis, by):
    length = lax.axis_size(axis)
    pairs = [(i, i + by) for i in range(length) if 0 <= i + by < length]
    return lax.ppermute(shard, axis, pairs)


def attend_heads(projected):
    total_rows = projected.shape[0]
    block = min(512, total_rows)
    factor = projected.shape[-1] ** (-0.5)
    outputs = []
    for begin_row in range(0, total_rows, block):
        end_row = begin_row + block
        query_rows = projected[begin_row:end_row, :, 0, :]
        key_rows = projected[:end_row, :, 1, :]
        value_rows = projected[:end_row, :, 2, :]
        scores = (
            jnp.einsum("qhe,khe->hqk", query_rows, key_rows, preferred_element_type=jnp.float32)
            * factor
        )
        row_place = begin_row + lax.broadcasted_iota(jnp.int32, (block, end_row), 0)
        col_place = lax.broadcasted_iota(jnp.int32, (block, end_row), 1)
        scores = jnp.where(col_place <= row_place, scores, -jnp.inf)
        row_max = jnp.max(scores, axis=-1, keepdims=True)
        raw_weights = jnp.exp(scores - row_max)
        attention = (raw_weights / jnp.sum(raw_weights, axis=-1, keepdims=True)).astype(
            jnp.bfloat16
        )
        outputs.append(
            jnp.einsum(
                "hqk,khe->qhe", attention, value_rows, preferred_element_type=jnp.float32
            ).astype(jnp.bfloat16)
        )
    return jnp.concatenate(outputs, axis=0)


def local(stream, depth_weights, depth_reach, norm_gain, qkv_weight):
    own_block = stream[0]
    spacing = lax.axis_size("section") // 4
    coefficients = depth_weights[0]
    reach_here = depth_reach[0]
    depth_mix = coefficients[0] * own_block.astype(jnp.float32)
    for distance in range(1, 4):
        earlier = shifted(own_block, "section", distance * spacing)
        weight_now = jnp.where(distance <= reach_here, coefficients[distance], 0.0)
        depth_mix = depth_mix + weight_now * earlier.astype(jnp.float32)
    layer_input = depth_mix.astype(jnp.bfloat16)
    mean_square = jnp.mean(depth_mix * depth_mix, axis=-1, keepdims=True)
    normed = (depth_mix * lax.rsqrt(mean_square + 1e-05) * norm_gain[0]).astype(jnp.bfloat16)
    local_weight = qkv_weight[0]
    projected = jnp.einsum(
        "rd,dhce->rhce",
        lax.all_gather(normed, "seq", axis=0, tiled=True),
        local_weight,
        preferred_element_type=jnp.float32,
    ).astype(jnp.bfloat16)
    attended = attend_heads(projected)
    regrouped = lax.all_to_all(attended, "seq", split_axis=0, concat_axis=1, tiled=True)
    return (
        layer_input[None],
        regrouped.reshape(1, regrouped.shape[0], regrouped.shape[1] * regrouped.shape[2]),
    )


def solution(mesh):
    placed = (
        P("section", "seq", None),
        P("section", None),
        P("section"),
        P("section", None),
        P("section", None, "seq", None, None),
    )
    return jax.shard_map(
        local,
        mesh=mesh,
        in_specs=placed,
        out_specs=(P("section", "seq", None), P("section", "seq", None)),
        check_vma=False,
    )
```

profile of v0, /device:TPU:17, one launch (start us, length us, event | category | flops | bytes accessed | tf_op | source)
XLA Modules:
  0.0 372.1 jit_solution(9795431878517355923)
XLA Ops:
  7.2 0.0 all-gather.2.cloned.1.call-start
  7.2 0.7 collective-permute-start.2
  7.9 1.3 collective-permute-start.1
  9.2 3.5 collective-permute-start
  13.4 1.5 fusion.60
  16.7 0.0 collective-permute-done.2
  16.7 19.4 %collective-permute-done.1 = bf16[128,4096]{1,0:T(8,128)(2,1)S(1)} collective-permute-done((bf16[128,4096]{1,0:T(8,128)(2,1)}, bf16[128,4096]{1,0:T(8,128)(2,1)S(1)}, u32[]{:S(2)}, u32[]{:S(2)}) %collective-permute-start.1) | collective-permute-done | bytes 1048608 | tf_op jit(solution)/shard_map/ppermute | solution.py:10
  36.1 23.5 %collective-permute-done = bf16[128,4096]{1,0:T(8,128)(2,1)S(1)} collective-permute-done((bf16[128,4096]{1,0:T(8,128)(2,1)}, bf16[128,4096]{1,0:T(8,128)(2,1)S(1)}, u32[]{:S(2)}, u32[]{:S(2)}) %collective-permute-start) | collective-permute-done | bytes 1048608 | tf_op jit(solution)/shard_map/ppermute | solution.py:10
  59.6 0.0 copy-start.4
  59.6 2.8 multiply_reduce_fusion
  62.4 0.0 copy-done.4
  62.4 1.7 multiply_convert_fusion
  64.1 0.0 all-gather.2.cloned.1.call-update
  64.2 0.1 iota_compare_fusion.3
  64.2 1.2 iota_compare_fusion.2
  65.4 1.6 iota_compare_fusion
  67.0 1.4 iota_compare_fusion.1
  68.4 199.0 %all-gather.2.cloned.1.call-done = bf16[2048,4096]{1,0:T(8,128)(2,1)} async-done(((bf16[128,4096]{1,0:T(8,128)(2,1)}), bf16[2048,4096]{1,0:T(8,128)(2,1)}) %all-gather.2.cloned.1.call-update) | async-done | bytes 16777232 | tf_op jit(solution)/shard_map/all_gather | solution.py:59
  267.4 18.2 %fusion.13 = bf16[2048,2,3,128]{3,0,2,1:T(8,128)(2,1)S(1)} fusion(bf16[4096,2,3,128]{3,1,2,0:T(2,128)(2,1)} %bitcast.115, bf16[2048,4096]{1,0:T(8,128)(2,1)} %all-gather.2.cloned.1.call-done), kind=kOutput, calls=%fused_computation.23 | convolution fusion | flops 12886474752 | bytes 26214400 | tf_op jit(solution)/shard_map/rd,dhce->rhce/dot_general | solution.py:57
  285.7 4.6 %fusion.35 = f32[2,512,2048]{2,1,0:T(8,128)} fusion(bf16[2048,2,3,128]{3,0,2,1:T(8,128)(2,1)S(1)} %fusion.13), kind=kOutput, calls=%fused_computation.51 | convolution fusion | flops 536870912 | bytes 9699328 | tf_op jit(solution)/shard_map/qhe,khe->hqk/dot_general | solution.py:24
  290.3 2.7 fusion.42
  293.0 3.5 fusion.62
  296.4 5.1 %fusion.34 = bf16[512,2,128]{0,2,1:T(8,128)(2,1)} fusion(f32[2,512]{1,0:T(2,128)S(1)} %fusion.62, bf16[2048,2,3,128]{3,0,2,1:T(8,128)(2,1)S(1)} %fusion.13, pred[512,1536]{1,0:T(8,128)(4,1)} %iota_compare_fusion.1), kind=kOutput, calls=%fused_computation.49 | convolution fusion | flops 813304320 | bytes 2887680 | tf_op jit(solution)/shard_map/hqk,khe->qhe/dot_general | solution.py:36
  301.5 0.9 fusion.64
  302.4 1.9 fusion.32
  304.4 13.6 %fusion.61 = (f32[2,512]{1,0:T(2,128)S(1)}, f32[2,512,2048]{2,1,0:T(8,128)}) fusion(f32[2,512,2048]{2,1,0:T(8,128)} %fusion.35, pred[512,2048]{1,0:T(8,128)(4,1)} %iota_compare_fusion), kind=kOutput, calls=%fused_computation.90 | output fusion | flops 12584959 | bytes 17829888 | tf_op jit(solution)/shard_map/sub | solution.py:31
  318.0 0.0 copy-start
  318.0 0.0 copy-start.1
  318.0 5.1 %fusion.33 = bf16[512,2,128]{0,2,1:T(8,128)(2,1)S(1)} fusion(f32[2,512,2048]{2,1,0:T(8,128)} %get-tuple-element.11, f32[2,512]{1,0:T(2,128)S(1)} %get-tuple-element.10, bf16[2048,2,3,128]{3,0,2,1:T(8,128)(2,1)S(1)} %fusion.13), kind=kOutput, calls=%fused_computation.48 | convolution fusion | flops 541196288 | bytes 9703424 | tf_op jit(solution)/shard_map/hqk,khe->qhe/dot_general | solution.py:36
  323.1 0.0 copy-done
  323.1 0.0 copy-done.1
  323.2 2.0 fusion.63
  325.1 0.0 copy-start.2
  325.1 0.0 copy-start.3
  325.2 1.0 fusion.31
  326.1 0.0 copy-done.2
  326.1 0.0 copy-done.3
  326.2 0.1 pad_maximum_fusion
  326.3 0.8 copy.20
  327.1 35.9 %all_to_all.15 = bf16[2048,2,128]{2,1,0:T(2,128)(2,1)S(1)} all-to-all(bf16[2048,2,128]{2,1,0:T(2,128)(2,1)S(1)} %copy.20), channel_id=1, replica_groups=mesh['section'=16,'seq'=16] {'seq'}, dimensions={0} | all-to-all | bytes 2097152 | tf_op jit(solution)/shard_map/all_to_all | solution.py:64
  363.0 0.7 copy.21
  363.7 1.6 reshape.38
  (4 shorter events, 0.0 us)
Async XLA Ops:
  7.2 260.3 %all-gather.2.cloned.1.call-start = ((), (), s32[]{:S(2)}) async-start(), calls=%async_computation.1 | async-start | bytes 17825792 | tf_op jit(solution)/shard_map/all_gather | solution.py:59
  7.2 9.5 %collective-permute-start.2 = (bf16[128,4096]{1,0:T(8,128)(2,1)}, bf16[128,4096]{1,0:T(8,128)(2,1)S(1)}, u32[]{:S(2)}, u32[]{:S(2)}) collective-permute-start(bf16[128,4096]{1,0:T(8,128)(2,1)} %bitcast.111), channel_id=1, source_target_pairs={{0,192},{16,208},{32,224},{48,240},{1,193},{17,209},{33,225},{49,2... | collective-permute-start | bytes 3145736 | tf_op jit(solution)/shard_map/ppermute | solution.py:10
  7.9 28.1 %collective-permute-start.1 = (bf16[128,4096]{1,0:T(8,128)(2,1)}, bf16[128,4096]{1,0:T(8,128)(2,1)S(1)}, u32[]{:S(2)}, u32[]{:S(2)}) collective-permute-start(bf16[128,4096]{1,0:T(8,128)(2,1)} %bitcast.112), channel_id=1, source_target_pairs={{0,128},{16,144},{32,160},{48,176},{64,192},{80,208},{96,224},{112... | collective-permute-start | bytes 3145736 | tf_op jit(solution)/shard_map/ppermute | solution.py:10
  9.2 50.3 %collective-permute-start = (bf16[128,4096]{1,0:T(8,128)(2,1)}, bf16[128,4096]{1,0:T(8,128)(2,1)S(1)}, u32[]{:S(2)}, u32[]{:S(2)}) collective-permute-start(bf16[128,4096]{1,0:T(8,128)(2,1)} %bitcast.113), channel_id=1, source_target_pairs={{0,64},{16,80},{32,96},{48,112},{64,128},{80,144},{96,160},{112,17... | collective-permute-start | bytes 3145736 | tf_op jit(solution)/shard_map/ppermute | solution.py:10
  59.6 2.9 copy-start.4
  318.0 5.1 %copy-start = (f32[2,512,1024]{2,1,0:T(8,128)S(1)}, f32[2,512,1024]{2,1,0:T(8,128)}, u32[]{:S(2)}) copy-start(f32[2,512,1024]{2,1,0:T(8,128)} %fusion.42) | copy-start | bytes 12582916
  318.0 5.2 %copy-start.1 = (pred[512,1024]{1,0:T(8,128)(4,1)S(1)}, pred[512,1024]{1,0:T(8,128)(4,1)}, u32[]{:S(2)}) copy-start(pred[512,1024]{1,0:T(8,128)(4,1)} %iota_compare_fusion.2) | copy-start | bytes 1572868
  325.1 1.0 copy-start.2
  325.1 1.0 copy-start.3
Sparse Core Ops, SparseCore 0:
  64.2 203.1 all-gather.1
where the time goes:
time: 374 us; the launch traced here: 372 us
  waiting for transfers between devices  242 us (65%)
  matrix products  43 us (11%)
  blocking collectives  35.9 us (10%)
  other arithmetic  24.5 us (7%)
  between operations  16.7 us (4%)
  starting transfers between devices  5.53 us (1%)
  local copies, waits for them, and re-layouts  4.63 us (1%)
    all_gather x1, waiting for transfers between devices, local(): lax.all_gather(normed, 'seq', axis=0, tiled=True)  199 us
    ppermute x3, waiting for transfers between devices, shifted(): return lax.ppermute(shard, axis, pairs)  42.8 us
    all_to_all x1, blocking collectives, local(): lax.all_to_all(attended, 'seq', split_axis=0, concat_axis=1, tiled=True)  35.9 us
    dot_general x1, matrix products, local(): jnp.einsum('rd,dhce->rhce', lax.all_gather(normed, 'seq', axis=0, tiled=T...  18.2 us
    sub x2, other arithmetic, attend_heads(): raw_weights = jnp.exp(scores - row_max)  15.6 us
    dot_general x4, matrix products, attend_heads(): jnp.einsum('hqk,khe->qhe', attention, value_rows, preferred_element_type=...  13.1 us
  transfers between devices with their start and end apart: 4, of which 3 were waited for; matrix products, arithmetic and copies ran while one was open for 2% of the time, Pallas kernels for 0%

commit v1 on v0

v1 whole, which is shorter than its diff:
```python
import jax
import jax.numpy as jnp
from jax import lax
from jax.experimental import pallas as pl
from jax.experimental.pallas import tpu as pltpu
from jax.sharding import PartitionSpec as P

MESH = pl.DeviceIdType.MESH
SIDE = 4
PEERS = SIDE * SIDE
CHUNKS = 8
ROWS = 16
SPACING = 4
REACH = 3
D = 4096
HD = 128
SPLIT = 3200


def wrap(value):
    return lax.rem(value + 2 * SIDE, SIDE)


def kernel(
    weights_ref, reach_ref, stream_ref, gain_ref, w_hbm,
    layer_ref, out_ref,
    gathered, earlier, w_ref, mix, qkv, attended,
    send_sem, recv_sem, depth_send, depth_recv, w_sem, out_send, out_recv, own_sem,
):
    section = lax.axis_index("section")
    me = lax.axis_index("seq")
    layer_y = section // SPACING
    x, z = me // SIDE, lax.rem(me, SIDE)

    w_copy = pltpu.make_async_copy(w_hbm, w_ref, w_sem)
    w_copy.start()

    barrier = pltpu.get_barrier_semaphore()
    for step in range(1, PEERS):
        pl.semaphore_signal(
            barrier, inc=1,
            device_id={"seq": lax.rem(me + step, PEERS)}, device_id_type=MESH,
        )
    for step in range(1, SIDE):
        pl.semaphore_signal(
            barrier, inc=1,
            device_id={"section": lax.rem(section + step * SPACING, SIDE * SPACING)},
            device_id_type=MESH,
        )
    pl.semaphore_wait(barrier, PEERS - 1 + SIDE - 1)

    def depth_copy(chunk, distance):
        return pltpu.make_async_remote_copy(
            src_ref=stream_ref.at[chunk],
            dst_ref=earlier.at[distance - 1, chunk],
            send_sem=depth_send.at[distance - 1, chunk],
            recv_sem=depth_recv.at[distance - 1, chunk],
            device_id={"section": lax.rem(section + distance * SPACING, SIDE * SPACING)},
            device_id_type=MESH,
        )

    def start_depth(chunk):
        for distance in range(1, REACH + 1):
            @pl.when(layer_y + distance < SIDE)
            def _():
                depth_copy(chunk, distance).start()

    def columns(part):
        return pl.ds(0, SPLIT) if part == 0 else pl.ds(SPLIT, D - SPLIT)

    def place(part, major, minor):
        return minor * SIDE + major if part == 0 else major * SIDE + minor

    def block_copy(part, chunk, origin, target):
        block = gathered.at[chunk, origin, :, columns(part)]
        return pltpu.make_async_remote_copy(
            src_ref=block,
            dst_ref=block,
            send_sem=send_sem.at[part, chunk],
            recv_sem=recv_sem.at[part, chunk, origin],
            device_id={"seq": target},
            device_id_type=MESH,
        )

    def arrive(part, chunk, origin):
        block_copy(part, chunk, origin, lax.rem(me + 1, PEERS)).wait_recv()

    spots = ((z, x), (x, z))

    def own(chunk):
        for distance in range(1, REACH + 1):
            @pl.when(layer_y >= distance)
            def _():
                depth_copy(chunk, distance).wait_recv()
        mix[...] = weights_ref[0, 0] * stream_ref[chunk].astype(jnp.float32)
        for distance in range(1, REACH + 1):
            @pl.when(layer_y >= distance)
            def _():
                now = jnp.where(distance <= reach_ref[0], weights_ref[0, distance], 0.0)
                mix[...] += now * earlier[distance - 1, chunk].astype(jnp.float32)
        value = mix[...]
        layer_ref[chunk] = value.astype(jnp.bfloat16)
        square = jnp.mean(value * value, axis=-1, keepdims=True)
        gathered[chunk, me] = (value * lax.rsqrt(square + 1e-05) * gain_ref[...]).astype(
            jnp.bfloat16
        )
        for part in (0, 1):
            major, minor = spots[part]
            for by in (1, -1):
                block_copy(part, chunk, me, place(part, wrap(major + by), minor)).start()
            for by in (1, -1):
                block_copy(part, chunk, me, place(part, major, wrap(minor + by))).start()

    def turn_of(chunk):
        return 1 - 2 * lax.rem(chunk, 2)

    def spread(chunk):
        turn = turn_of(chunk)
        for index, by in enumerate((-1, 1, 2)):
            for part in (0, 1):
                major, minor = spots[part]
                origin = place(part, wrap(major + by * turn), minor)
                arrive(part, chunk, origin)
                if index == 0:
                    block_copy(part, chunk, origin, place(part, wrap(major + turn), minor)).start()
                for side in (1, -1):
                    block_copy(
                        part, chunk, origin, place(part, major, wrap(minor + side))
                    ).start()

    rows_of = ((0, 1), (-1, -1), (1, -1), (2, 1))

    def relay(chunk):
        turn = turn_of(chunk)
        for by, way in rows_of:
            for part in (0, 1):
                major, minor = spots[part]
                row = wrap(major + by * turn)
                origin = place(part, row, wrap(minor - way * turn))
                arrive(part, chunk, origin)
                block_copy(
                    part, chunk, origin, place(part, major, wrap(minor + way * turn))
                ).start()

    def finish(chunk):
        turn = turn_of(chunk)
        for by, way in rows_of:
            for part in (0, 1):
                major, minor = spots[part]
                row = wrap(major + by * turn)
                arrive(part, chunk, place(part, row, wrap(minor + way * turn)))
                arrive(part, chunk, place(part, row, wrap(minor + 2)))
        block = gathered[chunk].reshape(PEERS * ROWS, D)
        for tile in range(3):
            product = jnp.dot(
                block, w_ref[:, tile * 256:(tile + 1) * 256],
                preferred_element_type=jnp.float32,
            ).astype(jnp.bfloat16)
            for half in range(2):
                qkv[2 * tile + half, :, chunk] = product[
                    :, half * HD:(half + 1) * HD
                ].reshape(PEERS, ROWS, HD)

    for chunk in range(2):
        start_depth(chunk)

    @pl.loop(0, CHUNKS + 3)
    def _(step):
        @pl.when(step < CHUNKS)
        def _():
            own(step)

        @pl.when(step + 2 < CHUNKS)
        def _():
            start_depth(step + 2)

        @pl.when((step >= 1) & (step < CHUNKS + 1))
        def _():
            spread(step - 1)

        @pl.when((step >= 2) & (step < CHUNKS + 2))
        def _():
            relay(step - 2)

        @pl.when(step == 3)
        def _():
            w_copy.wait()

        @pl.when(step >= 3)
        def _():
            finish(step - 3)

    scale = (HD ** -0.5) * 1.4426950408889634
    across = (((1,), (1,)), ((), ()))

    def attend(block):
        size = 2 * CHUNKS * ROWS
        row = lax.broadcasted_iota(jnp.int32, (size, size), 0)
        column = lax.broadcasted_iota(jnp.int32, (size, size), 1)
        for head in range(2):
            query = qkv[3 * head, 2 * block:2 * block + 2].reshape(size, HD)
            pieces = [(2 * block, 2 * block + 2)]
            if block > 0:
                pieces.append((0, 2 * block))
            scores = []
            for begin, end in pieces:
                key = qkv[3 * head + 1, begin:end].reshape((end - begin) * HD, HD)
                scores.append(
                    lax.dot_general(query, key, across, preferred_element_type=jnp.float32)
                )
            scores[0] = jnp.where(column <= row, scores[0], -jnp.inf)
            top = jnp.max(scores[0], axis=-1, keepdims=True)
            if block > 0:
                top = jnp.maximum(top, jnp.max(scores[1], axis=-1, keepdims=True))
            total, result = 0.0, 0.0
            for (begin, end), score in zip(pieces, scores):
                raw = jnp.exp2((score - top) * scale)
                total = total + jnp.sum(raw, axis=-1, keepdims=True)
                value = qkv[3 * head + 2, begin:end].reshape((end - begin) * HD, HD)
                result = result + jnp.dot(
                    raw.astype(jnp.bfloat16), value, preferred_element_type=jnp.float32
                )
            attended[2 * block:2 * block + 2, :, head * HD:(head + 1) * HD] = (
                (result / total).astype(jnp.bfloat16).reshape(2, HD, HD)
            )

    lanes = out_ref.at[:, pl.ds(pl.multiple_of(me * 2 * HD, 2 * HD), 2 * HD)]
    keep = pltpu.make_async_copy(attended.at[me], lanes, own_sem)

    @pl.loop(0, PEERS // 2)
    def _(step):
        block = lax.rem(me // 2 + 1 + step, PEERS // 2)
        for variant in range(PEERS // 2):
            @pl.when(block == variant)
            def _():
                attend(variant)
        for half in range(2):
            target = 2 * block + half

            @pl.when(target != me)
            def _():
                pltpu.make_async_remote_copy(
                    src_ref=attended.at[target],
                    dst_ref=lanes,
                    send_sem=out_send,
                    recv_sem=out_recv,
                    device_id={"seq": target},
                    device_id_type=MESH,
                ).start()

    keep.start()
    for part in (0, 1):
        @pl.loop(0, CHUNKS)
        def _(chunk):
            sent = gathered.at[chunk, pl.ds(0, PEERS - 1), :, columns(part)]
            pltpu.make_async_copy(sent, sent, send_sem.at[part, chunk]).wait()
    for distance in range(1, REACH + 1):
        @pl.when(layer_y + distance < SIDE)
        def _():
            @pl.loop(0, CHUNKS)
            def _(chunk):
                depth_copy(chunk, distance).wait_send()
    keep.wait()
    moved = attended.at[pl.ds(0, PEERS - 1)]
    pltpu.make_async_copy(moved, moved, out_send).wait()
    pltpu.make_async_copy(moved, moved, out_recv).wait()


def local(stream, depth_weights, depth_reach, norm_gain, qkv_weight):
    vmem = pl.BlockSpec(memory_space=pltpu.VMEM)
    smem = pl.BlockSpec(memory_space=pltpu.SMEM)
    layer, attended = pl.pallas_call(
        kernel,
        out_shape=(
            jax.ShapeDtypeStruct((CHUNKS, ROWS, D), jnp.bfloat16),
            jax.ShapeDtypeStruct((CHUNKS * ROWS, D), jnp.bfloat16),
        ),
        in_specs=[smem, smem, vmem, vmem, pl.BlockSpec(memory_space=pl.ANY)],
        out_specs=(vmem, vmem),
        scratch_shapes=[
            pltpu.VMEM((CHUNKS, PEERS, ROWS, D), jnp.bfloat16),
            pltpu.VMEM((REACH, CHUNKS, ROWS, D), jnp.bfloat16),
            pltpu.VMEM((D, 6 * HD), jnp.bfloat16),
            pltpu.VMEM((ROWS, D), jnp.float32),
            pltpu.VMEM((6, PEERS, CHUNKS, ROWS, HD), jnp.bfloat16),
            pltpu.VMEM((PEERS, HD, 2 * HD), jnp.bfloat16),
            pltpu.SemaphoreType.DMA((2, CHUNKS)),
            pltpu.SemaphoreType.DMA((2, CHUNKS, PEERS)),
            pltpu.SemaphoreType.DMA((REACH, CHUNKS)),
            pltpu.SemaphoreType.DMA((REACH, CHUNKS)),
            pltpu.SemaphoreType.DMA,
            pltpu.SemaphoreType.DMA,
            pltpu.SemaphoreType.DMA,
            pltpu.SemaphoreType.DMA,
        ],
        compiler_params=pltpu.CompilerParams(
            collective_id=0, has_side_effects=True, vmem_limit_bytes=56 * 1024 * 1024
        ),
        cost_estimate=pl.CostEstimate(
            flops=16_000_000_000, bytes_accessed=12_000_000, transcendentals=5_000_000
        ),
    )(
        depth_weights, depth_reach,
        stream.reshape(CHUNKS, ROWS, D), norm_gain, qkv_weight.reshape(D, 6 * HD),
    )
    return layer.reshape(stream.shape), attended[None]


def solution(mesh):
    placed = (
        P("section", "seq", None),
        P("section", None),
        P("section"),
        P("section", None),
        P("section", None, "seq", None, None),
    )
    return jax.shard_map(
        local,
        mesh=mesh,
        in_specs=placed,
        out_specs=(P("section", "seq", None), P("section", "seq", None)),
        check_vma=False,
    )
```

time: 374 us -> 223 us (0.60)
  the two profiles are of different devices: /device:TPU:17 before, /device:TPU:30 now
where the time goes in v1:
time: 223 us; the launch traced here: 222 us
  Pallas kernels  191 us (86%)
  local copies, waits for them, and re-layouts  29.4 us (13%)
    pallas_call x1, Pallas kernels, local(): pl.pallas_call(kernel, out_shape=(jax.ShapeDtypeStruct((CHUNKS, ROWS, D),...  191 us
    unnamed x3, local copies, waits for them, and re-layouts  20.7 us
    reshape x1, local copies, waits for them, and re-layouts, local(): qkv_weight.reshape(D, 6 * HD)  8.67 us

profile of v1, /device:TPU:30, one launch (start us, length us, event | category | flops | bytes accessed | tf_op | source)
XLA Modules:
  0.0 222.1 jit_solution(3990378810690954238)
XLA Ops:
  0.6 16.2 %copy.8 = bf16[1,4096,2,3,128]{1,4,3,2,0:T(8,128)(2,1)} copy(bf16[1,4096,2,3,128]{4,2,3,1,0:T(2,128)(2,1)} %param.9) | data formatting | bytes 12582912 | tf_op args[4]
  16.8 8.7 %copy.9.w_hbm = bf16[4096,768]{1,0:T(8,128)(2,1)} copy(bf16[4096,768]{0,1:T(8,128)(2,1)} %bitcast.4) | data formatting | bytes 12582912 | tf_op jit(solution)/shard_map/reshape | solution.py:304
  26.1 191.4 %shard_map.68 = (bf16[8,16,4096]{2,1,0:T(8,128)(2,1)}, bf16[128,4096]{1,0:T(8,128)(2,1)}) custom-call(f32[1,4]{1,0:T(1,128)} %weights_ref.1, s32[1]{0:T(128)S(6)} %copy.12.reach_ref, bf16[8,16,4096]{2,1,0:T(8,128)(2,1)} %bitcast.7, f32[1,4096]{1,0:T(1,128)} %gain_ref.1, bf16[4096,768]{1,0:T(8,128)(2,1)} %copy.9.w_hbm), custom_call_target="tpu_custom_call" | custom-call | flops 16000000000 | bytes 12000000 | tf_op jit(solution)/shard_map/pallas_call | solution.py:272
  217.6 2.3 %copy.13 = bf16[1,128,4096]{2,1,0:T(8,128)(2,1)} copy(bf16[1,128,4096]{2,1,0:T(8,128)(2,1)} %bitcast.6) | data formatting | bytes 2097152
  219.9 2.3 %copy.14 = bf16[1,128,4096]{2,1,0:T(8,128)(2,1)} copy(bf16[1,128,4096]{2,1,0:T(8,128)(2,1)} %bitcast.5) | data formatting | bytes 2097152

commit v2 on v1

v2 whole, which is shorter than its diff:
```python
import jax
import jax.numpy as jnp
from jax import lax
from jax.experimental import pallas as pl
from jax.experimental.pallas import tpu as pltpu
from jax.sharding import PartitionSpec as P

MESH = pl.DeviceIdType.MESH
SIDE = 4
PEERS = SIDE * SIDE
CHUNKS = 8
ROWS = 16
SPACING = 4
REACH = 3
D = 4096
HD = 128
W_ROWS = 256
PIECES = 4
HEAD_START = 2
PARTS = 1
UNITS = CHUNKS * PARTS
WIDTH = D // PARTS
SPLIT = 3328


def wrap(value):
    return lax.rem(value + 2 * SIDE, SIDE)


def kernel(
    weights_ref, reach_ref, stream_ref, gain_ref, w_hbm,
    layer_ref, out_ref,
    gathered, earlier, w_raw, w_wide, w_ref, layer, mix, qkv, attended,
    send_sem, recv_sem, depth_send, depth_recv, w_sem, out_send, out_recv, own_sem, layer_sem, turn_sem,
):
    section = lax.axis_index("section")
    me = lax.axis_index("seq")
    layer_y = section // SPACING
    x, z = me // SIDE, lax.rem(me, SIDE)

    w_copy = pltpu.make_async_copy(w_hbm, w_raw, w_sem)
    w_copy.start()

    barrier = pltpu.get_barrier_semaphore()
    for step in range(1, PEERS):
        pl.semaphore_signal(
            barrier, inc=1,
            device_id={"seq": lax.rem(me + step, PEERS)}, device_id_type=MESH,
        )
    for step in range(1, SIDE):
        pl.semaphore_signal(
            barrier, inc=1,
            device_id={"section": lax.rem(section + step * SPACING, SIDE * SPACING)},
            device_id_type=MESH,
        )
    mate = section + 1 - 2 * lax.rem(section, 2)
    pl.semaphore_signal(barrier, inc=1, device_id={"section": mate}, device_id_type=MESH)
    pl.semaphore_wait(barrier, PEERS - 1 + SIDE - 1 + 1)
    leads = lax.rem(section, 2) == 0

    def depth_copy(chunk, distance):
        return pltpu.make_async_remote_copy(
            src_ref=stream_ref.at[chunk],
            dst_ref=earlier.at[distance - 1, chunk],
            send_sem=depth_send.at[distance - 1, chunk],
            recv_sem=depth_recv.at[distance - 1, chunk],
            device_id={"section": lax.rem(section + distance * SPACING, SIDE * SPACING)},
            device_id_type=MESH,
        )

    def start_depth(chunk):
        for distance in range(1, REACH + 1):
            @pl.when(layer_y + distance < SIDE)
            def _():
                depth_copy(chunk, distance).start()

    def layer_copy(chunk):
        return pltpu.make_async_copy(layer.at[chunk], layer_ref.at[chunk], layer_sem.at[chunk])

    def columns(part, unit, fold=None):
        begin = lax.rem(unit, PARTS) * WIDTH + (0 if part == 0 else SPLIT)
        size = SPLIT if part == 0 else WIDTH - SPLIT
        if fold is not None:
            near = size // 256 * 128
            begin, size = (begin, near) if fold == 0 else (begin + near, size - near)
        return pl.ds(pl.multiple_of(begin, 128), size)

    def place(part, major, minor):
        return minor * SIDE + major if part == 0 else major * SIDE + minor

    def block_copy(part, unit, origin, target, fold=None):
        block = gathered.at[unit // PARTS, origin, :, columns(part, unit, fold)]
        return pltpu.make_async_remote_copy(
            src_ref=block,
            dst_ref=block,
            send_sem=send_sem.at[part, unit],
            recv_sem=recv_sem.at[part, unit, PEERS if fold == 1 else origin],
            device_id={"seq": target},
            device_id_type=MESH,
        )

    def arrive(part, unit, origin, fold=None):
        block_copy(part, unit, origin, lax.rem(me + 1, PEERS), fold).wait_recv()

    spots = ((z, x), (x, z))

    def mix_rows(chunk):
        for distance in range(1, REACH + 1):
            @pl.when(layer_y >= distance)
            def _():
                depth_copy(chunk, distance).wait_recv()
        mix[...] = weights_ref[0, 0] * stream_ref[chunk].astype(jnp.float32)
        for distance in range(1, REACH + 1):
            @pl.when(layer_y >= distance)
            def _():
                now = jnp.where(distance <= reach_ref[0], weights_ref[0, distance], 0.0)
                mix[...] += now * earlier[distance - 1, chunk].astype(jnp.float32)
        value = mix[...]
        layer[chunk] = value.astype(jnp.bfloat16)
        layer_copy(chunk).start()
        square = jnp.mean(value * value, axis=-1, keepdims=True)
        gathered[chunk, me] = (value * lax.rsqrt(square + 1e-05) * gain_ref[...]).astype(
            jnp.bfloat16
        )
    def own(unit):
        @pl.when(lax.rem(unit, PARTS) == 0)
        def _():
            mix_rows(unit // PARTS)

        for part in (0, 1):
            major, minor = spots[part]
            for by in (1, -1):
                block_copy(part, unit, me, place(part, wrap(major + by), minor)).start()
            for by in (1, -1):
                block_copy(part, unit, me, place(part, major, wrap(minor + by))).start()

    def aside(part, unit, origin):
        major, minor = spots[part]
        for side in (1, -1):
            block_copy(part, unit, origin, place(part, major, wrap(minor + side))).start()

    def spread_near(unit):
        for part in (0, 1):
            major, minor = spots[part]
            for fold, by in enumerate((-1, 1)):
                origin = place(part, wrap(major + by), minor)
                arrive(part, unit, origin)
                block_copy(part, unit, origin, place(part, wrap(major - by), minor), fold).start()
                aside(part, unit, origin)

    def spread_far(unit):
        for part in (0, 1):
            major, minor = spots[part]
            origin = place(part, wrap(major + 2), minor)
            for fold in (0, 1):
                arrive(part, unit, origin, fold)
            aside(part, unit, origin)

    rows_of = ((0, 1), (-1, -1), (1, -1), (2, 1))

    def relay(unit, rows):
        for by, way in rows:
            for part in (0, 1):
                major, minor = spots[part]
                origin = place(part, wrap(major + by), wrap(minor - way))
                arrive(part, unit, origin)
                block_copy(part, unit, origin, place(part, major, wrap(minor + way))).start()

    def finish(unit):
        for by, way in rows_of:
            for part in (0, 1):
                major, minor = spots[part]
                row = wrap(major + by)
                arrive(part, unit, place(part, row, wrap(minor + way)))
                arrive(part, unit, place(part, row, wrap(minor + 2)))

        @pl.when(lax.rem(unit, PARTS) == PARTS - 1)
        def _():
            project(unit // PARTS)

    def project(chunk):
        block = gathered[chunk].reshape(PEERS * ROWS, D)
        for tile in range(3):
            product = jnp.dot(
                block, w_ref[:, tile * 256:(tile + 1) * 256],
                preferred_element_type=jnp.float32,
            ).astype(jnp.bfloat16)
            for half in range(2):
                qkv[2 * tile + half, :, chunk] = product[
                    :, half * HD:(half + 1) * HD
                ].reshape(PEERS, ROWS, HD)

    @pl.when(jnp.logical_not(leads))
    def _():
        pl.semaphore_wait(turn_sem, 1)

    start_depth(0)

    w_copy.wait()

    @pl.loop(0, D // W_ROWS)
    def _(part):
        begin = pl.multiple_of(part * W_ROWS, W_ROWS)
        w_wide[...] = w_raw[pl.ds(pl.multiple_of(part * W_ROWS * 6, W_ROWS * 6), W_ROWS * 6)].astype(
            jnp.float32
        )
        for piece in range(6):
            w_ref[pl.ds(begin, W_ROWS), piece * HD:(piece + 1) * HD] = w_wide[
                pl.ds(piece, W_ROWS, stride=6)
            ].astype(jnp.bfloat16)

    start_depth(1)

    @pl.loop(0, UNITS + 4)
    def _(step):
        def when(lag, work):
            @pl.when((step >= lag) & (step < UNITS + lag))
            def _():
                work(step - lag)

        when(0, own)

        @pl.when((lax.rem(step, PARTS) == 0) & (step // PARTS + 2 < CHUNKS))
        def _():
            start_depth(step // PARTS + 2)

        when(1, spread_near)
        when(2, lambda unit: relay(unit, rows_of[:3]))

        @pl.when(leads & (step == HEAD_START))
        def _():
            pl.semaphore_signal(turn_sem, inc=1, device_id={"section": mate}, device_id_type=MESH)

        when(2, spread_far)
        when(3, lambda unit: relay(unit, rows_of[3:]))
        when(4, finish)

    scale = (HD ** -0.5) * 1.4426950408889634
    across = (((1,), (1,)), ((), ()))

    def attend(block):
        size = 2 * CHUNKS * ROWS
        row = lax.broadcasted_iota(jnp.int32, (size, size), 0)
        column = lax.broadcasted_iota(jnp.int32, (size, size), 1)
        for head in range(2):
            query = qkv[head, 2 * block:2 * block + 2].reshape(size, HD)
            pieces = [(2 * block, 2 * block + 2)]
            if block > 0:
                pieces.append((0, 2 * block))
            scores = []
            for begin, end in pieces:
                key = qkv[2 + head, begin:end].reshape((end - begin) * HD, HD)
                scores.append(
                    lax.dot_general(query, key, across, preferred_element_type=jnp.float32)
                )
            scores[0] = jnp.where(column <= row, scores[0], -jnp.inf)
            top = jnp.max(scores[0], axis=-1, keepdims=True)
            if block > 0:
                top = jnp.maximum(top, jnp.max(scores[1], axis=-1, keepdims=True))
            total, result = 0.0, 0.0
            for (begin, end), score in zip(pieces, scores):
                raw = jnp.exp2((score - top) * scale)
                total = total + jnp.sum(raw, axis=-1, keepdims=True)
                value = qkv[4 + head, begin:end].reshape((end - begin) * HD, HD)
                result = result + jnp.dot(
                    raw.astype(jnp.bfloat16), value, preferred_element_type=jnp.float32
                )
            attended[2 * block:2 * block + 2, :, head * HD:(head + 1) * HD] = (
                (result / total).astype(jnp.bfloat16).reshape(2, HD, HD)
            )

    lanes = out_ref.at[:, pl.ds(pl.multiple_of(me * 2 * HD, 2 * HD), 2 * HD)]
    keep = pltpu.make_async_copy(attended.at[me], lanes, own_sem)

    @pl.loop(0, PEERS // 2)
    def _(step):
        block = lax.rem(me // 2 + 1 + step, PEERS // 2)
        for variant in range(PEERS // 2):
            @pl.when(block == variant)
            def _():
                attend(variant)
        for half in range(2):
            target = 2 * block + half

            @pl.when(target != me)
            def _():
                pltpu.make_async_remote_copy(
                    src_ref=attended.at[target],
                    dst_ref=lanes,
                    send_sem=out_send,
                    recv_sem=out_recv,
                    device_id={"seq": target},
                    device_id_type=MESH,
                ).start()

    keep.start()
    for part in (0, 1):
        @pl.loop(0, UNITS)
        def _(unit):
            sent = gathered.at[unit // PARTS, pl.ds(0, PEERS - 1), :, columns(part, unit)]
            pltpu.make_async_copy(sent, sent, send_sem.at[part, unit]).wait()
    for distance in range(1, REACH + 1):
        @pl.when(layer_y + distance < SIDE)
        def _():
            @pl.loop(0, CHUNKS)
            def _(chunk):
                depth_copy(chunk, distance).wait_send()
    @pl.loop(0, CHUNKS)
    def _(chunk):
        layer_copy(chunk).wait()

    keep.wait()
    moved = attended.at[pl.ds(0, PEERS - 1)]
    pltpu.make_async_copy(moved, moved, out_send).wait()
    pltpu.make_async_copy(moved, moved, out_recv).wait()


def hand_over(layer, attended, layer_out, attended_out):
    layer_out[...] = layer[...]
    attended_out[...] = attended[...]


def local(stream, depth_weights, depth_reach, norm_gain, qkv_weight):
    vmem = pl.BlockSpec(memory_space=pltpu.VMEM)
    smem = pl.BlockSpec(memory_space=pltpu.SMEM)
    layer, attended = pl.pallas_call(
        kernel,
        out_shape=(
            jax.ShapeDtypeStruct((CHUNKS, ROWS, D), jnp.bfloat16),
            jax.ShapeDtypeStruct((CHUNKS * ROWS, D), jnp.bfloat16),
        ),
        in_specs=[smem, smem, vmem, vmem, pl.BlockSpec(memory_space=pl.ANY)],
        out_specs=(pl.BlockSpec(memory_space=pl.ANY),) * 2,
        scratch_shapes=[
            pltpu.VMEM((CHUNKS, PEERS, ROWS, D), jnp.bfloat16),
            pltpu.VMEM((REACH, CHUNKS, ROWS, D), jnp.bfloat16),
            pltpu.VMEM((D * 6, HD), jnp.bfloat16),
            pltpu.VMEM((W_ROWS * 6, HD), jnp.float32),
            pltpu.VMEM((D, 6 * HD), jnp.bfloat16),
            pltpu.VMEM((CHUNKS, ROWS, D), jnp.bfloat16),
            pltpu.VMEM((ROWS, D), jnp.float32),
            pltpu.VMEM((6, PEERS, CHUNKS, ROWS, HD), jnp.bfloat16),
            pltpu.VMEM((PEERS, HD, 2 * HD), jnp.bfloat16),
            pltpu.SemaphoreType.DMA((2, UNITS)),
            pltpu.SemaphoreType.DMA((2, UNITS, PEERS + 1)),
            pltpu.SemaphoreType.DMA((REACH, CHUNKS)),
            pltpu.SemaphoreType.DMA((REACH, CHUNKS)),
            pltpu.SemaphoreType.DMA,
            pltpu.SemaphoreType.DMA,
            pltpu.SemaphoreType.DMA,
            pltpu.SemaphoreType.DMA,
            pltpu.SemaphoreType.DMA((CHUNKS,)),
            pltpu.SemaphoreType.REGULAR,
        ],
        compiler_params=pltpu.CompilerParams(
            collective_id=0, has_side_effects=True, vmem_limit_bytes=56 * 1024 * 1024
        ),
        cost_estimate=pl.CostEstimate(
            flops=16_000_000_000, bytes_accessed=12_000_000, transcendentals=5_000_000
        ),
    )(
        depth_weights, depth_reach,
        stream.reshape(CHUNKS, ROWS, D), norm_gain, jnp.transpose(qkv_weight[0], (0, 2, 1, 3)).reshape(D * 6, HD),
    )
    layer, attended = pl.pallas_call(
        hand_over,
        out_shape=(jax.ShapeDtypeStruct((CHUNKS * ROWS, D), jnp.bfloat16),) * 2,
        grid=(PIECES,),
        in_specs=[pl.BlockSpec((CHUNKS * ROWS // PIECES, D), lambda i: (i, 0))] * 2,
        out_specs=(pl.BlockSpec((CHUNKS * ROWS // PIECES, D), lambda i: (i, 0)),) * 2,
    )(layer.reshape(CHUNKS * ROWS, D), attended)
    return layer[None], attended[None]


def solution(mesh):
    placed = (
        P("section", "seq", None),
        P("section", None),
        P("section"),
        P("section", None),
        P("section", None, "seq", None, None),
    )
    return jax.shard_map(
        local,
        mesh=mesh,
        in_specs=placed,
        out_specs=(P("section", "seq", None), P("section", "seq", None)),
        check_vma=False,
    )
```

time: 223 us -> 174 us (0.78)
  the two profiles are of different devices: /device:TPU:30 before, /device:TPU:17 now
where the time goes in v2:
time: 174 us
  Pallas kernels  172 us (99%)
    pallas_call x1, Pallas kernels, local(): pl.pallas_call(kernel, out_shape=(jax.ShapeDtypeStruct((CHUNKS, ROWS, D),...  169 us
    pallas_call x1, Pallas kernels, local(): pl.pallas_call(hand_over, out_shape=(jax.ShapeDtypeStruct((CHUNKS * ROWS,...  3.75 us

profile of v2, /device:TPU:17, one launch (start us, length us, event | category | flops | bytes accessed | tf_op | source)
XLA Modules:
  0.0 173.7 jit_solution(9366632148794710394)
XLA Ops:
  1.3 168.7 %shard_map.68 = (bf16[8,16,4096]{2,1,0:T(8,128)(2,1)}, bf16[128,4096]{1,0:T(8,128)(2,1)}) custom-call(f32[1,4]{1,0:T(1,128)} %weights_ref.1, s32[1]{0:T(128)S(6)} %copy.7.reach_ref, bf16[8,16,4096]{2,1,0:T(8,128)(2,1)} %bitcast.11, f32[1,4096]{1,0:T(1,128)} %gain_ref.1, bf16[24576,128]{1,0:T(8,128)(2,1)} %bitcast.10), custom_call_target="tpu_custom_call" | custom-call | flops 16000000000 | bytes 12000000 | tf_op jit(solution)/shard_map/pallas_call | solution.py:326
  170.0 3.8 %shard_map.69 = (bf16[128,4096]{1,0:T(8,128)(2,1)}, bf16[128,4096]{1,0:T(8,128)(2,1)}) custom-call(bf16[128,4096]{1,0:T(8,128)(2,1)} %bitcast.9, bf16[128,4096]{1,0:T(8,128)(2,1)} %get-tuple-element.7.attended), custom_call_target="tpu_custom_call" | custom-call | tf_op jit(solution)/shard_map/pallas_call | solution.py:365

commit v3 on v2

--- a/solution.py
+++ b/solution.py
@@ -15,12 +15,12 @@
 D = 4096
 HD = 128
 W_ROWS = 256
-PIECES = 4
-HEAD_START = 2
-PARTS = 1
+LAGS = (2, 4, 6, 8)
+HEAD_START = 6
+PARTS = 2
 UNITS = CHUNKS * PARTS
 WIDTH = D // PARTS
-SPLIT = 3328
+SPLIT = 1664
 
 
 def wrap(value):
@@ -28,19 +28,16 @@
 
 
 def kernel(
-    weights_ref, reach_ref, stream_ref, gain_ref, w_hbm,
+    weights_ref, reach_ref, stream_hbm, gain_ref, w_hbm,
     layer_ref, out_ref,
-    gathered, earlier, w_raw, w_wide, w_ref, layer, mix, qkv, attended,
-    send_sem, recv_sem, depth_send, depth_recv, w_sem, out_send, out_recv, own_sem, layer_sem, turn_sem,
+    stream_ref, gathered, earlier, w_raw, w_wide, w_ref, mix, qkv, attended,
+    send_sem, recv_sem, depth_send, depth_recv, w_sem, out_send, out_recv, own_sem, stream_sem, turn_sem,
 ):
     section = lax.axis_index("section")
     me = lax.axis_index("seq")
     layer_y = section // SPACING
     x, z = me // SIDE, lax.rem(me, SIDE)
 
-    w_copy = pltpu.make_async_copy(w_hbm, w_raw, w_sem)
-    w_copy.start()
-
     barrier = pltpu.get_barrier_semaphore()
     for step in range(1, PEERS):
         pl.semaphore_signal(
@@ -55,6 +52,10 @@
         )
     mate = section + 1 - 2 * lax.rem(section, 2)
     pl.semaphore_signal(barrier, inc=1, device_id={"section": mate}, device_id_type=MESH)
+    stream_copy = pltpu.make_async_copy(stream_hbm, stream_ref, stream_sem)
+    stream_copy.start()
+    w_copy = pltpu.make_async_copy(w_hbm, w_raw, w_sem)
+    w_copy.start()
     pl.semaphore_wait(barrier, PEERS - 1 + SIDE - 1 + 1)
     leads = lax.rem(section, 2) == 0
 
@@ -73,9 +74,6 @@
             @pl.when(layer_y + distance < SIDE)
             def _():
                 depth_copy(chunk, distance).start()
-
-    def layer_copy(chunk):
-        return pltpu.make_async_copy(layer.at[chunk], layer_ref.at[chunk], layer_sem.at[chunk])
 
     def columns(part, unit, fold=None):
         begin = lax.rem(unit, PARTS) * WIDTH + (0 if part == 0 else SPLIT)
@@ -116,8 +114,7 @@
                 now = jnp.where(distance <= reach_ref[0], weights_ref[0, distance], 0.0)
                 mix[...] += now * earlier[distance - 1, chunk].astype(jnp.float32)
         value = mix[...]
-        layer[chunk] = value.astype(jnp.bfloat16)
-        layer_copy(chunk).start()
+        layer_ref[chunk] = value.astype(jnp.bfloat16)
         square = jnp.mean(value * value, axis=-1, keepdims=True)
         gathered[chunk, me] = (value * lax.rsqrt(square + 1e-05) * gain_ref[...]).astype(
             jnp.bfloat16
@@ -190,6 +187,8 @@
                     :, half * HD:(half + 1) * HD
                 ].reshape(PEERS, ROWS, HD)
 
+    stream_copy.wait()
+
     @pl.when(jnp.logical_not(leads))
     def _():
         pl.semaphore_wait(turn_sem, 1)
@@ -211,7 +210,7 @@
 
     start_depth(1)
 
-    @pl.loop(0, UNITS + 4)
+    @pl.loop(0, UNITS + LAGS[3])
     def _(step):
         def when(lag, work):
             @pl.when((step >= lag) & (step < UNITS + lag))
@@ -224,16 +223,16 @@
         def _():
             start_depth(step // PARTS + 2)
 
-        when(1, spread_near)
-        when(2, lambda unit: relay(unit, rows_of[:3]))
+        when(LAGS[0], spread_near)
+        when(LAGS[1], lambda unit: relay(unit, rows_of[:3]))
 
         @pl.when(leads & (step == HEAD_START))
         def _():
             pl.semaphore_signal(turn_sem, inc=1, device_id={"section": mate}, device_id_type=MESH)
 
-        when(2, spread_far)
-        when(3, lambda unit: relay(unit, rows_of[3:]))
-        when(4, finish)
+        when(LAGS[1], spread_far)
+        when(LAGS[2], lambda unit: relay(unit, rows_of[3:]))
+        when(LAGS[3], finish)
 
     scale = (HD ** -0.5) * 1.4426950408889634
     across = (((1,), (1,)), ((), ()))
@@ -305,39 +304,31 @@
             @pl.loop(0, CHUNKS)
             def _(chunk):
                 depth_copy(chunk, distance).wait_send()
-    @pl.loop(0, CHUNKS)
-    def _(chunk):
-        layer_copy(chunk).wait()
-
     keep.wait()
     moved = attended.at[pl.ds(0, PEERS - 1)]
     pltpu.make_async_copy(moved, moved, out_send).wait()
     pltpu.make_async_copy(moved, moved, out_recv).wait()
 
 
-def hand_over(layer, attended, layer_out, attended_out):
-    layer_out[...] = layer[...]
-    attended_out[...] = attended[...]
-
-
 def local(stream, depth_weights, depth_reach, norm_gain, qkv_weight):
     vmem = pl.BlockSpec(memory_space=pltpu.VMEM)
     smem = pl.BlockSpec(memory_space=pltpu.SMEM)
+    hbm = pl.BlockSpec(memory_space=pl.ANY)
     layer, attended = pl.pallas_call(
         kernel,
         out_shape=(
-            jax.ShapeDtypeStruct((CHUNKS, ROWS, D), jnp.bfloat16),
-            jax.ShapeDtypeStruct((CHUNKS * ROWS, D), jnp.bfloat16),
+            pltpu.VMEM((CHUNKS, ROWS, D), jnp.bfloat16),
+            pltpu.VMEM((CHUNKS * ROWS, D), jnp.bfloat16),
         ),
-        in_specs=[smem, smem, vmem, vmem, pl.BlockSpec(memory_space=pl.ANY)],
-        out_specs=(pl.BlockSpec(memory_space=pl.ANY),) * 2,
+        in_specs=[smem, smem, hbm, vmem, hbm],
+        out_specs=(vmem,) * 2,
         scratch_shapes=[
+            pltpu.VMEM((CHUNKS, ROWS, D), jnp.bfloat16),
             pltpu.VMEM((CHUNKS, PEERS, ROWS, D), jnp.bfloat16),
             pltpu.VMEM((REACH, CHUNKS, ROWS, D), jnp.bfloat16),
             pltpu.VMEM((D * 6, HD), jnp.bfloat16),
             pltpu.VMEM((W_ROWS * 6, HD), jnp.float32),
             pltpu.VMEM((D, 6 * HD), jnp.bfloat16),
-            pltpu.VMEM((CHUNKS, ROWS, D), jnp.bfloat16),
             pltpu.VMEM((ROWS, D), jnp.float32),
             pltpu.VMEM((6, PEERS, CHUNKS, ROWS, HD), jnp.bfloat16),
             pltpu.VMEM((PEERS, HD, 2 * HD), jnp.bfloat16),
@@ -349,11 +340,11 @@
             pltpu.SemaphoreType.DMA,
             pltpu.SemaphoreType.DMA,
             pltpu.SemaphoreType.DMA,
-            pltpu.SemaphoreType.DMA((CHUNKS,)),
+            pltpu.SemaphoreType.DMA,
             pltpu.SemaphoreType.REGULAR,
         ],
         compiler_params=pltpu.CompilerParams(
-            collective_id=0, has_side_effects=True, vmem_limit_bytes=56 * 1024 * 1024
+            collective_id=0, has_side_effects=True, vmem_limit_bytes=58 * 1024 * 1024
         ),
         cost_estimate=pl.CostEstimate(
             flops=16_000_000_000, bytes_accessed=12_000_000, transcendentals=5_000_000
@@ -362,14 +353,7 @@
         depth_weights, depth_reach,
         stream.reshape(CHUNKS, ROWS, D), norm_gain, jnp.transpose(qkv_weight[0], (0, 2, 1, 3)).reshape(D * 6, HD),
     )
-    layer, attended = pl.pallas_call(
-        hand_over,
-        out_shape=(jax.ShapeDtypeStruct((CHUNKS * ROWS, D), jnp.bfloat16),) * 2,
-        grid=(PIECES,),
-        in_specs=[pl.BlockSpec((CHUNKS * ROWS // PIECES, D), lambda i: (i, 0))] * 2,
-        out_specs=(pl.BlockSpec((CHUNKS * ROWS // PIECES, D), lambda i: (i, 0)),) * 2,
-    )(layer.reshape(CHUNKS * ROWS, D), attended)
-    return layer[None], attended[None]
+    return layer.reshape(stream.shape), attended[None]
 
 
 def solution(mesh):

time: 174 us -> 171 us (0.983)
  Pallas kernels: 172 us -> 168 us
  local copies, waits for them, and re-layouts: 0 us -> 1.94 us
    pallas_call x2 -> x1, Pallas kernels: 172 us -> 168 us  [local(): pl.pallas_call(kernel, out_shape=(pltpu.VMEM((CHUNKS, ROWS, D), jnp.bfloa...]
    unnamed x0 -> x2, local copies, waits for them, and re-layouts: none -> 1.94 us
where the time goes in v3:
time: 171 us
  Pallas kernels  168 us (98%)
  local copies, waits for them, and re-layouts  1.94 us (1%)
    pallas_call x1, Pallas kernels, local(): pl.pallas_call(kernel, out_shape=(pltpu.VMEM((CHUNKS, ROWS, D), jnp.bfloa...  168 us

profile of v3, /device:TPU:17, one launch (start us, length us, event | category | flops | bytes accessed | tf_op | source)
XLA Modules:
  0.0 171.0 jit_solution(5407477037888283414)
XLA Ops:
  1.3 167.8 %shard_map.68 = (bf16[8,16,4096]{2,1,0:T(8,128)(2,1)S(1)}, bf16[128,4096]{1,0:T(8,128)(2,1)S(1)}) custom-call(f32[1,4]{1,0:T(1,128)} %weights_ref.1, s32[1]{0:T(128)S(6)} %copy.11.reach_ref, bf16[8,16,4096]{2,1,0:T(8,128)(2,1)} %bitcast.11, f32[1,4096]{1,0:T(1,128)} %gain_ref.1, bf16[24576,128]{1,0:T(8,128)(2,1)} %bitcast.10), custom_call_target="tpu_custom_call" | custom-call | flops 16000000000 | bytes 12000000 | tf_op jit(solution)/shard_map/pallas_call | solution.py:317
  169.1 1.0 copy.9
  170.0 1.0 copy.10

commit v4 on v3

--- a/solution.py
+++ b/solution.py
@@ -16,7 +16,7 @@
 HD = 128
 W_ROWS = 256
 LAGS = (2, 4, 6, 8)
-HEAD_START = 6
+HEAD_START = 7
 PARTS = 2
 UNITS = CHUNKS * PARTS
 WIDTH = D // PARTS

time: 171 us -> 171 us (level); the launches traced: 171 us -> 169 us
  Pallas kernels: 168 us -> 166 us
    pallas_call x1, Pallas kernels: 168 us -> 166 us  [local(): pl.pallas_call(kernel, out_shape=(pltpu.VMEM((CHUNKS, ROWS, D), jnp.bfloa...]
where the time goes in v4:
time: 171 us; the launch traced here: 169 us
  Pallas kernels  166 us (97%)
  local copies, waits for them, and re-layouts  1.94 us (1%)
    pallas_call x1, Pallas kernels, local(): pl.pallas_call(kernel, out_shape=(pltpu.VMEM((CHUNKS, ROWS, D), jnp.bfloa...  166 us

profile of v4, /device:TPU:17, one launch (start us, length us, event | category | flops | bytes accessed | tf_op | source)
XLA Modules:
  0.0 169.0 jit_solution(11984197034340560806)
XLA Ops:
  1.3 165.7 %shard_map.68 = (bf16[8,16,4096]{2,1,0:T(8,128)(2,1)S(1)}, bf16[128,4096]{1,0:T(8,128)(2,1)S(1)}) custom-call(f32[1,4]{1,0:T(1,128)} %weights_ref.1, s32[1]{0:T(128)S(6)} %copy.11.reach_ref, bf16[8,16,4096]{2,1,0:T(8,128)(2,1)} %bitcast.11, f32[1,4096]{1,0:T(1,128)} %gain_ref.1, bf16[24576,128]{1,0:T(8,128)(2,1)} %bitcast.10), custom_call_target="tpu_custom_call" | custom-call | flops 16000000000 | bytes 12000000 | tf_op jit(solution)/shard_map/pallas_call | solution.py:317
  167.0 1.0 copy.9
  168.0 1.0 copy.10
